TPU v7x, 512 devices: a whole 4x4x16 slice. The times are simulated.
512 devices in a mesh: span: 8 (over x, core), dom: 64 (over y, z).
Axes of the slice: x: 4, y: 4, z: 16, core: 2. Of those that a mesh axis runs over, the one named last changes fastest.
Arguments:
- krylov: float32 [20, 5, 32, 16384], P(None, None, 'span', 'dom'), may hold values from -75 to 75
- limiter: float32 [5, 32, 16384], P(None, 'span', 'dom'), may hold values from 0 to 1
- pseudo_diag: float32 [32, 16384], P('span', 'dom'), may hold values from 1 to 4
- face_states: float32 [2, 5, 32, 32768], P(None, None, 'span', 'dom'), may hold values from -2 to 13.5, as said below
- face_angle: float32 [32768], P('dom'), may hold values from -3.140625 to 3.140625
- face_area: float32 [32768], P('dom'), may hold values from 0.3 to 1.5
- slope_weight: float32 [32768], P('dom'), may hold values from 0.05 to 0.3
- span_coupling: float32 [16384], P('dom'), may hold values from 0.2 to 1
- face_cells: int32 [2, 32768], P(None, 'dom'), may hold values from 0 to 767, as said below
- send_list: int32 [4, 8192], P(None, 'dom'), may hold values from 0 to 255, as said below
- send_count: int32 [4, 64], P(None, 'dom'), may hold values from 0 to 128, as said below
Outputs:
- new_vectors: float32 [3, 5, 32, 16384], P(None, None, 'span', 'dom')
- hessenberg: float32 [3, 23], replicated
Inputs may be any that keep to these rules, and one draw needn't show every extreme that they name: `face_cells`: row 0 names owned cells, below 256. A row 1 entry at or above 256 is a ghost slot 256 + j * 128 + k that is live: its sender block exists and k is below that sender's send_count; every live slot of a block is named by exactly one face; a row 1 entry below 256 differs from row 0. `send_list`: entries of one peer slot's list of one block are distinct owned cells. `send_count`: A slot whose receiving block (dom index plus its offset) does not exist has count 0; some block sends a full 128 in slots 2 and 3. `face_states`: each saved state has density and pressure 0.5 or more.
All inputs are finite; a program needn't handle non-finite values.
Results may differ from a plain program's by a relative error of at most 0.00085.
Values sent between devices are 32-bit elements; how exact they have to be, the bound alone decides.
A program may use at most 64 MiB of HBM per device.

v0:
```python
import functools

import jax
import jax.numpy as jnp
from jax import lax
from jax.experimental import pallas as pl
from jax.experimental.pallas import tpu as pltpu
from jax.sharding import PartitionSpec as P

MESH = pl.DeviceIdType.MESH
OFFSETS = (-2, -1, 1, 2)
NEAR = (1, 2, 0, 3)
EPSILON = 1e-06
F32 = jnp.float32
BF16 = jnp.bfloat16
STEPS = 3
NVEC = 20
CELLS = 256
FACES = 512
CAP = 128


def dot_nn(a, b):
    return lax.dot_general(a, b, (((1,), (0,)), ((), ())), preferred_element_type=F32)


def dot_nt(a, b):
    return lax.dot_general(a, b, (((1,), (1,)), ((), ())), preferred_element_type=F32)


def iota(shape, dim):
    return lax.broadcasted_iota(jnp.int32, shape, dim)


def top_rows(shape):
    return (iota(shape, 0) & 4) == 0


def flip(x):
    return pltpu.roll(x, 4, 0)


def split2(x):
    hi = x.astype(BF16).astype(F32)
    return jnp.concatenate([hi, x - hi], axis=0)


def split3(x):
    hi = x.astype(BF16).astype(F32)
    rest = x - hi
    mid = rest.astype(BF16).astype(F32)
    return jnp.concatenate([hi, mid, rest - mid], axis=0)


def operand(fields):
    both = split2(jnp.concatenate(fields, axis=0))
    top = top_rows(both.shape)
    return jnp.concatenate([jnp.where(top, both, 0.0), jnp.where(top, 0.0, both)], axis=1).astype(BF16)


def joined(y):
    half = y.shape[0] // 2
    return y[:half] + y[half:]


def packed_cells(y):
    out = []
    for v in range(5):
        low, high = y[8 * v : 8 * v + 8, :CAP], y[8 * v : 8 * v + 8, CAP:]
        top = top_rows(low.shape)
        out.append(jnp.where(top, low, high) + flip(jnp.where(top, high, low)))
    return out


def one_hot(size, row):
    return (iota((size, row.shape[1]), 0) == row).astype(F32)


def kernel(
    grid,
    count,
    k_any,
    lim_any,
    pd_any,
    fs_any,
    pack_any,
    sl_any,
    nv_any,
    hess_ref,
    kv,
    limv,
    pdv,
    fsv,
    packv,
    slv,
    nvs,
    sv,
    rv,
    w_own,
    w_sc,
    w_nb,
    cf_int,
    cf_gf,
    pl_int,
    pl_gf,
    msg_out,
    msg_in,
    nbuf,
    sbuf,
    gbuf,
    abuf,
    load_sem,
    out_sem,
    msg_send,
    msg_recv,
    nb_send,
    nb_recv,
    sp_send,
    sp_recv,
    g_send,
    g_recv,
    a_send,
    a_recv,
):
    ns, ny, nz = grid
    nd = ny * nz
    s = lax.axis_index("span")
    d = lax.axis_index("dom")
    y, z = d // nz, lax.rem(d, nz)

    def dom_at(offset):
        return lax.rem(d + (offset + nd), nd)

    def span_at(offset):
        return lax.rem(s + (offset + ns), ns)

    groups = (
        (ns, s, lambda t: (t, d)),
        (ny, y, lambda t: (s, t * nz + z)),
        (nz, z, lambda t: (s, y * nz + t)),
    )
    starts = (0, ns, ns + ny)

    loads = [
        pltpu.make_async_copy(src, dst, load_sem.at[i])
        for i, (src, dst) in enumerate(
            (
                (pack_any, packv),
                (fs_any, fsv),
                (sl_any, slv),
                (k_any, kv),
                (lim_any, limv),
                (pd_any, pdv),
            )
        )
    ]
    for load in loads:
        load.start()

    barrier = pltpu.get_barrier_semaphore()
    partners = 0
    for o in OFFSETS:
        pl.semaphore_signal(barrier, inc=1, device_id=(s, dom_at(o)), device_id_type=MESH)
        partners += 1
    for n, me, device in groups:
        for k in range(1, n):
            pl.semaphore_signal(barrier, inc=1, device_id=device(lax.rem(me + k, n)), device_id_type=MESH)
            partners += 1

    def send_field(src, number):
        copies = []
        for j in NEAR:
            copy = pltpu.make_async_remote_copy(
                src_ref=src,
                dst_ref=nbuf.at[number, 3 - j],
                send_sem=nb_send.at[number, j],
                recv_sem=nb_recv.at[number, 3 - j],
                device_id=(s, dom_at(OFFSETS[j])),
                device_id_type=MESH,
            )
            copy.start()
            copies.append((j, copy))
        return dict(copies)

    def send_span(src, number):
        copies = []
        for side, offset in ((0, 1), (1, -1)):
            copy = pltpu.make_async_remote_copy(
                src_ref=src,
                dst_ref=sbuf.at[number, side],
                send_sem=sp_send.at[number, side],
                recv_sem=sp_recv.at[number, side],
                device_id=(span_at(offset), d),
                device_id_type=MESH,
            )
            copy.start()
            copies.append(copy)
        return copies

    unsent = []

    def sum_start(buf, send, recv, stage, value):
        n, me, device = groups[stage]
        buf[pl.ds(starts[stage] + me, 1)] = value[None]
        for k in range(1, n):
            place = buf.at[starts[stage] + me]
            pltpu.make_async_remote_copy(
                src_ref=place,
                dst_ref=place,
                send_sem=send.at[stage],
                recv_sem=recv.at[stage],
                device_id=device(lax.rem(me + k, n)),
                device_id_type=MESH,
            ).start()
        span = buf.at[pl.ds(starts[stage], n - 1)]
        unsent.append(pltpu.make_async_copy(span, span, send.at[stage]))

    def sum_finish(buf, recv, stage):
        n = groups[stage][0]
        span = buf.at[pl.ds(starts[stage], n - 1)]
        pltpu.make_async_copy(span, span, recv.at[stage]).wait()
        total = buf[starts[stage]]
        for k in range(1, n):
            total = total + buf[starts[stage] + k]
        return total

    loads[0].wait()
    loads[1].wait()
    angle, area, weight = packv[0:1, :], packv[1:2, :], packv[2:3, :]
    owner = packv[3:4, :].astype(jnp.int32)
    other = packv[4:5, :].astype(jnp.int32)
    nx, ny_ = jnp.cos(angle), jnp.sin(angle)
    state = [jnp.concatenate([fsv[0, v], fsv[1, v]], axis=0) for v in range(5)]
    inv = 1.0 / state[0]
    u1, u2, u3 = state[1] * inv, state[2] * inv, state[3] * inv
    pressure = 0.4 * (state[4] - 0.5 * (state[1] * u1 + state[2] * u2 + state[3] * u3))
    enthalpy = (state[4] + pressure) * inv
    speed = jnp.abs(u1 * nx + u2 * ny_) + jnp.sqrt(1.4 * pressure * inv)
    lam = jnp.maximum(speed, flip(speed))
    lam = jnp.where(top_rows(lam.shape), lam, -lam)
    half_area = 0.5 * area
    coefs = [u1, u2, u3, enthalpy, lam]
    for i, c in enumerate(coefs):
        cf_int[i] = c
    inside = (other < CELLS).astype(F32)
    pl_int[0:1, :] = nx
    pl_int[1:2, :] = ny_
    pl_int[2:3, :] = half_area * inside
    pl_int[3:4, :] = weight * inside
    pl_int[4:8, :] = jnp.zeros((4, FACES), F32)

    loads[2].wait()
    plane_rows = jnp.concatenate(
        [nx, ny_, half_area, weight, packv[3:4, :], jnp.zeros((3, FACES), F32)], axis=0
    )
    gathered = split3(jnp.concatenate([*coefs, plane_rows], axis=0)).astype(BF16)
    for j in range(4):
        slots = (iota((CAP, FACES), 0) + (CELLS + j * CAP) == other).astype(F32).astype(BF16)
        part = dot_nt(gathered, slots)
        part = part[0:48] + part[48:96] + part[96:144]
        msg_out[j, 0:45, :] = part[0:45]
        msg_out[j, 45:46, :] = slv[3 - j : 4 - j, :].astype(F32)
        msg_out[j, 46:48, :] = jnp.zeros((2, CAP), F32)

    loads[3].wait()
    pl.semaphore_wait(barrier, partners)

    first = send_field(kv.at[pl.ds(40 * NVEC - 40, 40)], 0)
    messages = {}
    for j in NEAR:
        copy = pltpu.make_async_remote_copy(
            src_ref=msg_out.at[j],
            dst_ref=msg_in.at[j],
            send_sem=msg_send.at[j],
            recv_sem=msg_recv.at[j],
            device_id=(s, dom_at(-OFFSETS[j])),
            device_id_type=MESH,
        )
        copy.start()
        messages[j] = copy
    first_span = send_span(kv.at[pl.ds(40 * NVEC - 40, 40)], 0)

    total = jnp.zeros((72, 72), F32)
    for pair in range(20):
        rows = jnp.concatenate(
            [kv[pl.ds(2 * pair + i, NVEC, stride=40), :] for i in range(2)], axis=1
        )
        rows = jnp.concatenate([rows, jnp.zeros((4, 2 * CAP), F32)], axis=0)
        rows = split3(rows).astype(BF16)
        total = total + dot_nt(rows, rows)
    rows = total[0:24] + total[24:48] + total[48:72]
    gram = rows[:, 0:24] + rows[:, 24:48] + rows[:, 48:72]
    gram = jnp.concatenate([gram, jnp.zeros((24, CAP - 24), F32)], axis=1)
    gram = gram[0:8] + pltpu.roll(gram[8:16], 32, 1) + pltpu.roll(gram[16:24], 64, 1)
    sum_start(gbuf, g_send, g_recv, 0, gram)

    hot_a, hot_b = one_hot(CELLS, owner), one_hot(CELLS, other)
    w_own[:, 0:512] = (hot_a - hot_b).astype(BF16)
    w_sc[:, 0:512] = hot_a.astype(BF16)
    w_sc[:, 512:1024] = hot_b.astype(BF16)
    for j in range(4):
        at = 512 + j * CAP
        hot = one_hot(CELLS, msg_out[j, 44:45, :].astype(jnp.int32)).astype(BF16)
        w_own[:, at : at + CAP] = hot
        w_sc[:, at + 512 : at + 512 + CAP] = hot
        hot = one_hot(CELLS, slv[j : j + 1, :])
        w_own[:, at + 512 : at + 512 + CAP] = (-hot).astype(BF16)
        w_sc[:, at + 1024 : at + 1024 + CAP] = hot.astype(BF16)

    gram = sum_finish(gbuf, g_recv, 0)
    sum_start(gbuf, g_send, g_recv, 1, gram)

    for j in NEAR:
        messages[j].wait_recv()
        at = j * CAP
        for i in range(5):
            mine, theirs = msg_out[j, 8 * i : 8 * i + 8, :], msg_in[j, 8 * i : 8 * i + 8, :]
            cf_gf[i, :, at : at + CAP] = jnp.where(top_rows(mine.shape), mine, theirs)
        for side, msg in ((0, msg_out), (1, msg_in)):
            pl_gf[side, :, at : at + CAP] = msg[j, 40:48, :]
        w_nb[j, :, 0:CAP] = (-one_hot(CELLS, msg_in[j, 45:46, :].astype(jnp.int32))).astype(BF16)
        w_nb[j, :, CAP:] = one_hot(CELLS, msg_in[j, 44:45, :].astype(jnp.int32)).astype(BF16)

    def jumps(own, number, copies):
        near = joined(dot_nn(operand(own), w_own[...]))
        ghost = [None] * 4
        foreign = [None] * 4
        for j in NEAR:
            copies[3 - j].wait_recv()
            part = joined(dot_nn(operand([nbuf[number, j]]), w_nb[j]))
            ghost[3 - j] = part[:, :CAP]
            foreign[j] = part[:, CAP:]
        return (
            near[:, 0:512],
            near[:, 512:1024] + jnp.concatenate(ghost, axis=1),
            near[:, 1024:1536] + jnp.concatenate(foreign, axis=1),
        )

    def transposed(e, cf, nx, ny, half_area):
        e = [half_area * x for x in e]
        u1, u2, u3, enthalpy, lam = (cf[i] for i in range(5))
        vn = u1 * nx + u2 * ny
        phi = 0.2 * (u1 * u1 + u2 * u2 + u3 * u3)
        cp = e[1] * nx + e[2] * ny + e[4] * vn
        ch = e[0] + e[1] * u1 + e[2] * u2 + e[3] * u3 + e[4] * enthalpy
        diag = vn + lam
        cp4 = 0.4 * cp
        return [
            e[0] * diag + cp * phi - ch * vn,
            e[1] * diag - u1 * cp4 + ch * nx,
            e[2] * diag - u2 * cp4 + ch * ny,
            e[3] * diag - u3 * cp4,
            e[4] * diag + cp4,
        ]

    def state_part(own, number, copies):
        e_int, e_gh, e_for = jumps(own, number, copies)
        jump_int, jump_gf = [], []
        for v in range(5):
            x = e_int[8 * v : 8 * v + 8]
            jump_int.append(x + flip(x))
            g, f = e_gh[8 * v : 8 * v + 8], e_for[8 * v : 8 * v + 8]
            top = top_rows(g.shape)
            jump_gf.append(jnp.where(top, g, f) + flip(jnp.where(top, f, g)))
        g_int = transposed(jump_int, cf_int, pl_int[0:1, :], pl_int[1:2, :], pl_int[2:3, :])
        top = top_rows((8, FACES))
        rows = [jnp.where(top, pl_gf[0, i : i + 1, :], pl_gf[1, i : i + 1, :]) for i in range(3)]
        g_gf = transposed(jump_gf, cf_gf, *rows)
        parts = []
        for g in (jnp.concatenate(g_int, axis=0), jnp.concatenate(g_gf, axis=0)):
            top = top_rows(g.shape)
            parts += [jnp.where(top, g, 0.0), jnp.where(top, 0.0, g)]
        lhs = split2(jnp.concatenate(parts, axis=1)).astype(BF16)
        return packed_cells(joined(dot_nt(lhs, w_sc[...])))

    def slope_part(own, number, copies):
        d_int, d_gh, d_for = jumps(own, number, copies)
        lhs = jnp.concatenate(
            [d_int * pl_int[3:4, :], d_gh * pl_gf[0, 3:4, :], d_for * pl_gf[1, 3:4, :]], axis=1
        )
        return packed_cells(joined(dot_nt(split2(lhs).astype(BF16), w_own[...])))

    row = iota((8, CAP), 0)
    layer = row & 3
    coupling = jnp.where(row < 4, packv[5:6, 0:CAP], packv[5:6, CAP : 2 * CAP])
    eye = iota((24, CAP), 0) == iota((24, CAP), 1)
    row24 = iota((24, CAP), 0)

    def row_of(column):
        return jnp.sum(jnp.where(eye, column, 0.0), axis=0, keepdims=True)

    def local_sums(terms):
        rows = []
        for i in range(24):
            if i in terms:
                rows.append(jnp.sum(terms[i], axis=0, keepdims=True))
            else:
                rows.append(jnp.zeros((1, CAP), F32))
        return row_of(jnp.sum(jnp.concatenate(rows, axis=0), axis=1, keepdims=True))

    def product(a, b):
        out = a[0] * b[0]
        for v in range(1, 5):
            out = out + a[v] * b[v]
        return out

    def basis(i):
        return [kv[40 * i + 8 * v : 40 * i + 8 * v + 8, :] for v in range(5)]

    q = basis(NVEC - 1)
    copies, span_copies = first, first_span
    inverse = None
    done = []
    rr = None
    hess = []
    for m in range(STEPS):
        state_terms = state_part(q, 2 * m, copies)
        if m == 0:
            gram = sum_finish(gbuf, g_recv, 1)
            sum_start(gbuf, g_send, g_recv, 2, gram)
            loads[4].wait()
            loads[5].wait()
        slope_field = [limv[v] * state_terms[v] for v in range(5)]
        sv[m] = jnp.concatenate(slope_field, axis=0)
        slope_copies = send_field(sv.at[m], 2 * m + 1)
        for copy in span_copies:
            copy.wait_recv()
        local = []
        for v in range(5):
            above = jnp.where(layer == 0, pltpu.roll(sbuf[m, 0, 8 * v : 8 * v + 8, :], 5, 0), pltpu.roll(q[v], 1, 0))
            below = jnp.where(layer == 3, pltpu.roll(sbuf[m, 1, 8 * v : 8 * v + 8, :], 3, 0), pltpu.roll(q[v], 7, 0))
            local.append(
                pdv[...] * q[v] + coupling * (2.0 * q[v] - above - below) + state_terms[v]
            )
        if m == 0:
            gram = sum_finish(gbuf, g_recv, 2) / count
            wide = jnp.concatenate(
                [gram, pltpu.roll(gram, CAP - 32, 1), pltpu.roll(gram, CAP - 64, 1)], axis=0
            )
            lane = iota((24, CAP), 1)
            kept = (lane < NVEC) & (row24 < NVEC)
            diagonal = (row24 == lane) & (row24 >= NVEC)
            work = jnp.where(kept, wide, 0.0) + jnp.where(diagonal | (lane == row24 + 32), 1.0, 0.0)
            for k in range(NVEC):
                column = jnp.sum(jnp.where(lane == k, work, 0.0), axis=1, keepdims=True)
                pivot = work[k : k + 1, :]
                scale = 1.0 / column[k : k + 1, :]
                work = work - (column - jnp.where(row24[:, 0:1] == k, 1.0, 0.0)) * (pivot * scale)
            inverse = pltpu.roll(work, CAP - 32, 1)
        slope_terms = slope_part(slope_field, 2 * m + 1, slope_copies)
        w = [local[v] - slope_terms[v] for v in range(5)]

        terms = {i: product(basis(i), w) for i in range(NVEC)}
        for i, vector in enumerate(done):
            terms[NVEC + i] = product(vector, w)
        if m:
            terms[NVEC + m - 1] = product(q, w)
            terms[22] = rr
        value = local_sums(terms)
        for stage in range(3):
            sum_start(abuf.at[m], a_send.at[m], a_recv.at[m], stage, value)
            value = sum_finish(abuf.at[m], a_recv.at[m], stage)
        solved = jnp.sum(inverse * (value / count), axis=1, keepdims=True)
        if m:
            beta = jnp.sqrt(solved[22:23, :] + EPSILON)
            scale = 1.0 / beta
            last = [x * scale for x in q]
            nvs[m - 1] = jnp.concatenate(last, axis=0)
            pltpu.make_async_copy(nvs.at[m - 1], nv_any.at[m - 1], out_sem.at[m - 1]).start()
            done.append(last)
            hess[-1] = jnp.where(iota((1, CAP), 1) == 22, beta, hess[-1])
            w = [x * scale for x in w]
            solved = solved * scale
            solved = jnp.where(row24[:, 0:1] == NVEC + m - 1, solved * scale, solved)
        hess.append(jnp.where(iota((1, CAP), 1) < NVEC + m, row_of(solved), 0.0))
        wide = jnp.broadcast_to(solved, (24, CAP))
        r = w
        for i in range(NVEC + m):
            c = wide[i : i + 1, :]
            vector = basis(i) if i < NVEC else done[i - NVEC]
            r = [r[v] - c * vector[v] for v in range(5)]
        rv[m] = jnp.concatenate(r, axis=0)
        if m + 1 < STEPS:
            copies = send_field(rv.at[m], 2 * m + 2)
            span_copies = send_span(rv.at[m], m + 1)
            unsent += [c.wait_send for c in (*copies.values(), *span_copies)]
        unsent += [c.wait_send for c in slope_copies.values()]
        rr = product(r, r)
        q = r

    value = local_sums({22: rr})
    for stage in range(3):
        sum_start(abuf.at[STEPS], a_send.at[STEPS], a_recv.at[STEPS], stage, value)
        value = sum_finish(abuf.at[STEPS], a_recv.at[STEPS], stage)
    beta = jnp.sqrt(value[:, 22:23] / count + EPSILON)
    scale = 1.0 / beta
    nvs[STEPS - 1] = jnp.concatenate([x * scale for x in q], axis=0)
    pltpu.make_async_copy(nvs.at[STEPS - 1], nv_any.at[STEPS - 1], out_sem.at[STEPS - 1]).start()
    hess[-1] = jnp.where(iota((1, CAP), 1) == 22, beta, hess[-1])
    hess_ref[...] = jnp.concatenate(hess, axis=0)[:, 0:23]

    for c in (*first.values(), *first_span, *messages.values()):
        c.wait_send()
    for c in unsent:
        if callable(c):
            c()
        else:
            c.wait()
    for m in range(STEPS):
        pltpu.make_async_copy(nvs.at[m], nv_any.at[m], out_sem.at[m]).wait()


def on_device(grid, krylov, limiter, pseudo_diag, face_states, face_angle, face_area, slope_weight,
              span_coupling, face_cells, send_list, send_count):
    ns, ny, nz = grid
    count = float(5 * 4 * CELLS * ns * ny * nz)

    def halves(x):
        lead = x.shape[:-2]
        x = x.reshape(*lead, 4, 2, CAP)
        return jnp.swapaxes(x, -3, -2).reshape(*lead, 8, CAP)

    pack = jnp.stack(
        [
            face_angle,
            face_area,
            slope_weight,
            face_cells[0].astype(F32),
            face_cells[1].astype(F32),
            jnp.pad(span_coupling, (0, FACES - CELLS)),
            jnp.zeros((FACES,), F32),
            jnp.zeros((FACES,), F32),
        ]
    )
    anywhere = pl.BlockSpec(memory_space=pl.ANY)
    members = ns + ny + nz
    dma = pltpu.SemaphoreType.DMA
    vectors, hess = pl.pallas_call(
        functools.partial(kernel, grid, count),
        out_shape=(
            jax.ShapeDtypeStruct((STEPS, 40, CAP), F32),
            jax.ShapeDtypeStruct((STEPS, 23), F32),
        ),
        in_specs=[anywhere] * 6,
        out_specs=(anywhere, pl.BlockSpec(memory_space=pltpu.VMEM)),
        scratch_shapes=[
            pltpu.VMEM((NVEC * 40, CAP), F32),
            pltpu.VMEM((5, 8, CAP), F32),
            pltpu.VMEM((8, CAP), F32),
            pltpu.VMEM((2, 5, 4, FACES), F32),
            pltpu.VMEM((8, FACES), F32),
            pltpu.VMEM((4, CAP), jnp.int32),
            pltpu.VMEM((STEPS, 40, CAP), F32),
            pltpu.VMEM((STEPS, 40, CAP), F32),
            pltpu.VMEM((STEPS, 40, CAP), F32),
            pltpu.VMEM((CELLS, 1536), BF16),
            pltpu.VMEM((CELLS, 2048), BF16),
            pltpu.VMEM((4, CELLS, 2 * CAP), BF16),
            pltpu.VMEM((5, 8, FACES), F32),
            pltpu.VMEM((5, 8, FACES), F32),
            pltpu.VMEM((8, FACES), F32),
            pltpu.VMEM((2, 8, FACES), F32),
            pltpu.VMEM((4, 48, CAP), F32),
            pltpu.VMEM((4, 48, CAP), F32),
            pltpu.VMEM((2 * STEPS, 4, 40, CAP), F32),
            pltpu.VMEM((STEPS, 2, 40, CAP), F32),
            pltpu.VMEM((members, 8, CAP), F32),
            pltpu.VMEM((STEPS + 1, members, 1, CAP), F32),
            dma((6,)),
            dma((STEPS,)),
            dma((4,)),
            dma((4,)),
            dma((2 * STEPS, 4)),
            dma((2 * STEPS, 4)),
            dma((STEPS, 2)),
            dma((STEPS, 2)),
            dma((3,)),
            dma((3,)),
            dma((STEPS + 1, 3)),
            dma((STEPS + 1, 3)),
        ],
        compiler_params=pltpu.CompilerParams(
            collective_id=0, has_side_effects=True, vmem_limit_bytes=48 * 2**20
        ),
    )(halves(krylov).reshape(NVEC * 40, CAP), halves(limiter), halves(pseudo_diag), face_states, pack, send_list)
    vectors = jnp.swapaxes(vectors.reshape(STEPS, 5, 2, 4, CAP), 2, 3)
    return vectors.reshape(STEPS, 5, 4, CELLS), hess


def solution(mesh):
    ns, nd = mesh.shape["span"], mesh.shape["dom"]
    ny = 4 if nd >= 16 else 2
    return jax.shard_map(
        functools.partial(on_device, (ns, ny, nd // ny)),
        mesh=mesh,
        in_specs=(
            P(None, None, "span", "dom"),
            P(None, "span", "dom"),
            P("span", "dom"),
            P(None, None, "span", "dom"),
            P("dom"),
            P("dom"),
            P("dom"),
            P("dom"),
            P(None, "dom"),
            P(None, "dom"),
            P(None, "dom"),
        ),
        out_specs=(P(None, None, "span", "dom"), P()),
        check_vma=False,
    )
```

profile of v0, /device:TPU:1, one launch (start us, length us, event | category | flops | bytes accessed | tf_op | source)
XLA Modules:
  0.0 118.2 jit_solution(8730443852071282254)
XLA Ops:
  0.6 0.0 copy-start.9
  0.6 0.0 copy-start.5
  0.6 0.7 copy-done.9
  1.3 0.0 copy-done.5
  1.3 0.0 copy-start.6
  1.3 0.0 copy-start.7
  1.3 0.0 copy-start.8
  1.4 0.0 copy-start.2
  1.4 0.6 copy-done.6
  2.0 0.0 copy-done.7
  2.0 0.0 copy-done.8
  2.0 0.0 copy-start.3
  2.0 0.0 copy-start.4
  2.1 0.0 copy-done.2
  2.1 0.6 copy-done.3
  2.7 0.0 copy-done.4
  2.7 0.0 copy-start
  2.7 1.0 copy-done
  3.7 0.0 copy-start.1
  3.8 0.9 copy-done.1
  4.6 112.3 %shard_map.113 = (f32[3,40,128]{2,1,0:T(8,128)S(1)}, f32[3,23]{1,0:T(4,128)S(1)}) custom-call(f32[800,128]{1,0:T(8,128)S(1)} %bitcast.24, f32[5,8,128]{2,1,0:T(8,128)S(1)} %bitcast.26, f32[8,128]{1,0:T(8,128)S(1)} %bitcast.27, f32[2,5,4,512]{3,2,1,0:T(4,128)S(1)} %copy-done.1, f32[8,512]{1,0:T(8,128)S(1)} %stack.25.pack_any, s32[4,128]{1,0:T(4,128)S(1)} %copy-done.4), custom_call_target="tpu_custom_call" | custom-call | tf_op jit(solution)/shard_map/pallas_call | solution.py:538
  117.0 0.6 copy.18
  117.6 0.6 copy.19
  (4 shorter events, 0.0 us)
Async XLA Ops:
  0.6 0.7 copy-start.9
  0.6 0.7 copy-start.5
  1.3 0.7 copy-start.6
  1.3 0.7 copy-start.7
  1.3 0.7 copy-start.8
  1.4 0.7 copy-start.2
  2.0 0.7 copy-start.3
  2.0 0.7 copy-start.4
  2.7 1.0 copy-start
  3.7 0.9 copy-start.1
where the time goes:
time: 119 us; the launch traced here: 118 us
  Pallas kernels  112 us (94%)
  local copies, waits for them, and re-layouts  5.15 us (4%)
    pallas_call x1, Pallas kernels, on_device(): pl.pallas_call(functools.partial(kernel, grid, count), out_shape=(jax.Sha...  112 us
    unnamed x22, local copies, waits for them, and re-layouts  5.11 us

commit v1 on v0

--- a/solution.py
+++ b/solution.py
@@ -83,7 +83,11 @@
     lim_any,
     pd_any,
     fs_any,
-    pack_any,
+    angle_any,
+    area_any,
+    weight_any,
+    coupling_any,
+    cells_any,
     sl_any,
     nv_any,
     hess_ref,
@@ -91,7 +95,11 @@
     limv,
     pdv,
     fsv,
-    packv,
+    anglev,
+    areav,
+    weightv,
+    couplingv,
+    cellsv,
     slv,
     nvs,
     sv,
@@ -134,38 +142,58 @@
     def span_at(offset):
         return lax.rem(s + (offset + ns), ns)
 
-    groups = (
-        (ns, s, lambda t: (t, d)),
-        (ny, y, lambda t: (s, t * nz + z)),
-        (nz, z, lambda t: (s, y * nz + t)),
+    xs = ns // 2
+    x, core = s // 2, lax.rem(s, 2)
+    places = (s * ny + y, z)
+    sizes = (ns * ny, nz)
+    starts = (0, ns * ny)
+
+    def others(stage):
+        if stage:
+            hops = sorted(range(1, nz), key=lambda k: -min(k, nz - k))
+            return [(s, y * nz + lax.rem(z + k, nz)) for k in hops]
+        hops = [(i, c, k) for i in range(xs) for c in range(2) for k in range(ny)]
+        hops = sorted(hops, key=lambda h: -(min(h[0], xs - h[0]) + min(h[2], ny - h[2])))
+        return [
+            (lax.rem(x + i, xs) * 2 + lax.rem(core + c, 2), lax.rem(y + k, ny) * nz + z)
+            for i, c, k in hops
+            if (i, c, k) != (0, 0, 0)
+        ]
+
+    barrier = pltpu.get_barrier_semaphore()
+    partners = [(s, dom_at(o)) for o in OFFSETS] + others(0) + others(1)
+    for device in partners:
+        pl.semaphore_signal(barrier, inc=1, device_id=device, device_id_type=MESH)
+
+    pairs = (
+        (fs_any, fsv),
+        (angle_any, anglev),
+        (area_any, areav),
+        (weight_any, weightv),
+        (cells_any, cellsv),
+        (sl_any, slv),
+        (k_any, kv),
+        (coupling_any, couplingv),
+        (lim_any, limv),
+        (pd_any, pdv),
     )
-    starts = (0, ns, ns + ny)
-
-    loads = [
-        pltpu.make_async_copy(src, dst, load_sem.at[i])
-        for i, (src, dst) in enumerate(
-            (
-                (pack_any, packv),
-                (fs_any, fsv),
-                (sl_any, slv),
-                (k_any, kv),
-                (lim_any, limv),
-                (pd_any, pdv),
-            )
-        )
-    ]
+    loads = [pltpu.make_async_copy(src, dst, load_sem.at[i]) for i, (src, dst) in enumerate(pairs)]
     for load in loads:
         load.start()
 
-    barrier = pltpu.get_barrier_semaphore()
-    partners = 0
-    for o in OFFSETS:
-        pl.semaphore_signal(barrier, inc=1, device_id=(s, dom_at(o)), device_id_type=MESH)
-        partners += 1
-    for n, me, device in groups:
-        for k in range(1, n):
-            pl.semaphore_signal(barrier, inc=1, device_id=device(lax.rem(me + k, n)), device_id_type=MESH)
-            partners += 1
+    exists = [(d + o >= 0) & (d + o < nd) for o in OFFSETS]
+    for j in range(4):
+
+        @pl.when(jnp.logical_not(exists[j]))
+        def _():
+            msg_in[j] = jnp.zeros((48, CAP), F32)
+            for number in range(2 * STEPS):
+                nbuf[number, j] = jnp.zeros((40, CAP), F32)
+
+    def when(condition, action):
+        @pl.when(condition)
+        def _():
+            action()
 
     def send_field(src, number):
         copies = []
@@ -178,7 +206,7 @@
                 device_id=(s, dom_at(OFFSETS[j])),
                 device_id_type=MESH,
             )
-            copy.start()
+            when(exists[j], copy.start)
             copies.append((j, copy))
         return dict(copies)
 
@@ -200,35 +228,33 @@
     unsent = []
 
     def sum_start(buf, send, recv, stage, value):
-        n, me, device = groups[stage]
-        buf[pl.ds(starts[stage] + me, 1)] = value[None]
-        for k in range(1, n):
-            place = buf.at[starts[stage] + me]
+        place = buf.at[starts[stage] + places[stage]]
+        buf[pl.ds(starts[stage] + places[stage], 1)] = value[None]
+        for device in others(stage):
             pltpu.make_async_remote_copy(
                 src_ref=place,
                 dst_ref=place,
                 send_sem=send.at[stage],
                 recv_sem=recv.at[stage],
-                device_id=device(lax.rem(me + k, n)),
+                device_id=device,
                 device_id_type=MESH,
             ).start()
-        span = buf.at[pl.ds(starts[stage], n - 1)]
-        unsent.append(pltpu.make_async_copy(span, span, send.at[stage]))
+        span = buf.at[pl.ds(starts[stage], sizes[stage] - 1)]
+        unsent.append(pltpu.make_async_copy(span, span, send.at[stage]).wait)
 
     def sum_finish(buf, recv, stage):
-        n = groups[stage][0]
+        n = sizes[stage]
         span = buf.at[pl.ds(starts[stage], n - 1)]
         pltpu.make_async_copy(span, span, recv.at[stage]).wait()
-        total = buf[starts[stage]]
-        for k in range(1, n):
-            total = total + buf[starts[stage] + k]
-        return total
-
-    loads[0].wait()
-    loads[1].wait()
-    angle, area, weight = packv[0:1, :], packv[1:2, :], packv[2:3, :]
-    owner = packv[3:4, :].astype(jnp.int32)
-    other = packv[4:5, :].astype(jnp.int32)
+        terms = [buf[starts[stage] + k] for k in range(n)]
+        while len(terms) > 1:
+            terms = [sum(terms[i + 1 : i + 2], terms[i]) for i in range(0, len(terms), 2)]
+        return terms[0]
+
+    for load in loads[:5]:
+        load.wait()
+    angle, area, weight = anglev[...], areav[...], weightv[...]
+    owner, other = cellsv[0:1, :], cellsv[1:2, :]
     nx, ny_ = jnp.cos(angle), jnp.sin(angle)
     state = [jnp.concatenate([fsv[0, v], fsv[1, v]], axis=0) for v in range(5)]
     inv = 1.0 / state[0]
@@ -249,9 +275,9 @@
     pl_int[3:4, :] = weight * inside
     pl_int[4:8, :] = jnp.zeros((4, FACES), F32)
 
-    loads[2].wait()
+    loads[5].wait()
     plane_rows = jnp.concatenate(
-        [nx, ny_, half_area, weight, packv[3:4, :], jnp.zeros((3, FACES), F32)], axis=0
+        [nx, ny_, half_area, weight, owner.astype(F32), jnp.zeros((3, FACES), F32)], axis=0
     )
     gathered = split3(jnp.concatenate([*coefs, plane_rows], axis=0)).astype(BF16)
     for j in range(4):
@@ -262,10 +288,9 @@
         msg_out[j, 45:46, :] = slv[3 - j : 4 - j, :].astype(F32)
         msg_out[j, 46:48, :] = jnp.zeros((2, CAP), F32)
 
-    loads[3].wait()
-    pl.semaphore_wait(barrier, partners)
-
-    first = send_field(kv.at[pl.ds(40 * NVEC - 40, 40)], 0)
+    pl.semaphore_wait(barrier, len(partners))
+
+    first = send_field(k_any.at[pl.ds(40 * NVEC - 40, 40)], 0)
     messages = {}
     for j in NEAR:
         copy = pltpu.make_async_remote_copy(
@@ -273,13 +298,14 @@
             dst_ref=msg_in.at[j],
             send_sem=msg_send.at[j],
             recv_sem=msg_recv.at[j],
-            device_id=(s, dom_at(-OFFSETS[j])),
+            device_id=(s, dom_at(OFFSETS[3 - j])),
             device_id_type=MESH,
         )
-        copy.start()
+        when(exists[3 - j], copy.start)
         messages[j] = copy
-    first_span = send_span(kv.at[pl.ds(40 * NVEC - 40, 40)], 0)
-
+    first_span = send_span(k_any.at[pl.ds(40 * NVEC - 40, 40)], 0)
+
+    loads[6].wait()
     total = jnp.zeros((72, 72), F32)
     for pair in range(20):
         rows = jnp.concatenate(
@@ -311,7 +337,7 @@
     sum_start(gbuf, g_send, g_recv, 1, gram)
 
     for j in NEAR:
-        messages[j].wait_recv()
+        when(exists[j], messages[j].wait_recv)
         at = j * CAP
         for i in range(5):
             mine, theirs = msg_out[j, 8 * i : 8 * i + 8, :], msg_in[j, 8 * i : 8 * i + 8, :]
@@ -326,7 +352,7 @@
         ghost = [None] * 4
         foreign = [None] * 4
         for j in NEAR:
-            copies[3 - j].wait_recv()
+            when(exists[j], copies[3 - j].wait_recv)
             part = joined(dot_nn(operand([nbuf[number, j]]), w_nb[j]))
             ghost[3 - j] = part[:, :CAP]
             foreign[j] = part[:, CAP:]
@@ -382,7 +408,8 @@
 
     row = iota((8, CAP), 0)
     layer = row & 3
-    coupling = jnp.where(row < 4, packv[5:6, 0:CAP], packv[5:6, CAP : 2 * CAP])
+    loads[7].wait()
+    coupling = jnp.where(row < 4, couplingv[:, 0:CAP], couplingv[:, CAP:])
     eye = iota((24, CAP), 0) == iota((24, CAP), 1)
     row24 = iota((24, CAP), 0)
 
@@ -413,13 +440,12 @@
     done = []
     rr = None
     hess = []
+    norms = []
     for m in range(STEPS):
         state_terms = state_part(q, 2 * m, copies)
         if m == 0:
-            gram = sum_finish(gbuf, g_recv, 1)
-            sum_start(gbuf, g_send, g_recv, 2, gram)
-            loads[4].wait()
-            loads[5].wait()
+            loads[8].wait()
+            loads[9].wait()
         slope_field = [limv[v] * state_terms[v] for v in range(5)]
         sv[m] = jnp.concatenate(slope_field, axis=0)
         slope_copies = send_field(sv.at[m], 2 * m + 1)
@@ -433,14 +459,15 @@
                 pdv[...] * q[v] + coupling * (2.0 * q[v] - above - below) + state_terms[v]
             )
         if m == 0:
-            gram = sum_finish(gbuf, g_recv, 2) / count
+            gram = sum_finish(gbuf, g_recv, 1) / count
             wide = jnp.concatenate(
                 [gram, pltpu.roll(gram, CAP - 32, 1), pltpu.roll(gram, CAP - 64, 1)], axis=0
             )
             lane = iota((24, CAP), 1)
             kept = (lane < NVEC) & (row24 < NVEC)
             diagonal = (row24 == lane) & (row24 >= NVEC)
-            work = jnp.where(kept, wide, 0.0) + jnp.where(diagonal | (lane == row24 + 32), 1.0, 0.0)
+            gram_mean = jnp.where(kept, wide, 0.0)
+            work = gram_mean + jnp.where(diagonal | (lane == row24 + 32), 1.0, 0.0)
             for k in range(NVEC):
                 column = jnp.sum(jnp.where(lane == k, work, 0.0), axis=1, keepdims=True)
                 pivot = work[k : k + 1, :]
@@ -456,13 +483,18 @@
         if m:
             terms[NVEC + m - 1] = product(q, w)
             terms[22] = rr
+        if m == STEPS - 1:
+            terms[23] = product(w, w)
         value = local_sums(terms)
-        for stage in range(3):
+        for stage in range(2):
             sum_start(abuf.at[m], a_send.at[m], a_recv.at[m], stage, value)
             value = sum_finish(abuf.at[m], a_recv.at[m], stage)
-        solved = jnp.sum(inverse * (value / count), axis=1, keepdims=True)
+        value = value / count
+        solved = jnp.sum(inverse * value, axis=1, keepdims=True)
         if m:
-            beta = jnp.sqrt(solved[22:23, :] + EPSILON)
+            norms.append(solved[22:23, :])
+            ww = solved[23:24, :]
+            beta = jnp.sqrt(norms[-1] + EPSILON)
             scale = 1.0 / beta
             last = [x * scale for x in q]
             nvs[m - 1] = jnp.concatenate(last, axis=0)
@@ -472,6 +504,8 @@
             w = [x * scale for x in w]
             solved = solved * scale
             solved = jnp.where(row24[:, 0:1] == NVEC + m - 1, solved * scale, solved)
+            if m == 1:
+                across = solved[20:21, :]
         hess.append(jnp.where(iota((1, CAP), 1) < NVEC + m, row_of(solved), 0.0))
         wide = jnp.broadcast_to(solved, (24, CAP))
         r = w
@@ -480,32 +514,41 @@
             vector = basis(i) if i < NVEC else done[i - NVEC]
             r = [r[v] - c * vector[v] for v in range(5)]
         rv[m] = jnp.concatenate(r, axis=0)
+        unsent += [functools.partial(when, exists[j], c.wait_send) for j, c in slope_copies.items()]
         if m + 1 < STEPS:
             copies = send_field(rv.at[m], 2 * m + 2)
             span_copies = send_span(rv.at[m], m + 1)
-            unsent += [c.wait_send for c in (*copies.values(), *span_copies)]
-        unsent += [c.wait_send for c in slope_copies.values()]
-        rr = product(r, r)
+            unsent += [functools.partial(when, exists[j], c.wait_send) for j, c in copies.items()]
+            unsent += [c.wait_send for c in span_copies]
+            rr = product(r, r)
         q = r
 
-    value = local_sums({22: rr})
-    for stage in range(3):
-        sum_start(abuf.at[STEPS], a_send.at[STEPS], a_recv.at[STEPS], stage, value)
-        value = sum_finish(abuf.at[STEPS], a_recv.at[STEPS], stage)
-    beta = jnp.sqrt(value[:, 22:23] / count + EPSILON)
+    n0, n1 = (n / (n + EPSILON) for n in norms)
+    cross = across * (1.0 - n0) / jnp.sqrt(norms[1] + EPSILON)
+    lane = iota((24, CAP), 1)
+    whole = gram_mean + jnp.where((row24 == 20) & (lane == 20), n0, 0.0)
+    whole = whole + jnp.where((row24 == 21) & (lane == 21), n1, 0.0)
+    whole = whole + jnp.where((row24 + lane == 41) & (row24 >= 20) & (lane >= 20), cross, 0.0)
+    c_row = row_of(jnp.where(row24[:, 0:1] < 22, solved, 0.0))
+    p_row = value * scale
+    p_row = jnp.where(iota((1, CAP), 1) == 21, p_row * scale, p_row)
+    inner = jnp.sum(whole * c_row - jnp.where(eye, 2.0 * p_row, 0.0), axis=1, keepdims=True)
+    inner = jnp.where(row24[:, 0:1] < 22, inner * solved, 0.0)
+    rr = ww * scale * scale + jnp.sum(inner, axis=0, keepdims=True)
+    beta = jnp.sqrt(jnp.maximum(rr, 0.0) + EPSILON)
     scale = 1.0 / beta
     nvs[STEPS - 1] = jnp.concatenate([x * scale for x in q], axis=0)
     pltpu.make_async_copy(nvs.at[STEPS - 1], nv_any.at[STEPS - 1], out_sem.at[STEPS - 1]).start()
     hess[-1] = jnp.where(iota((1, CAP), 1) == 22, beta, hess[-1])
     hess_ref[...] = jnp.concatenate(hess, axis=0)[:, 0:23]
 
-    for c in (*first.values(), *first_span, *messages.values()):
+    for j in range(4):
+        when(exists[j], first[j].wait_send)
+        when(exists[3 - j], messages[j].wait_send)
+    for c in first_span:
         c.wait_send()
-    for c in unsent:
-        if callable(c):
-            c()
-        else:
-            c.wait()
+    for wait in unsent:
+        wait()
     for m in range(STEPS):
         pltpu.make_async_copy(nvs.at[m], nv_any.at[m], out_sem.at[m]).wait()
 
@@ -520,20 +563,8 @@
         x = x.reshape(*lead, 4, 2, CAP)
         return jnp.swapaxes(x, -3, -2).reshape(*lead, 8, CAP)
 
-    pack = jnp.stack(
-        [
-            face_angle,
-            face_area,
-            slope_weight,
-            face_cells[0].astype(F32),
-            face_cells[1].astype(F32),
-            jnp.pad(span_coupling, (0, FACES - CELLS)),
-            jnp.zeros((FACES,), F32),
-            jnp.zeros((FACES,), F32),
-        ]
-    )
     anywhere = pl.BlockSpec(memory_space=pl.ANY)
-    members = ns + ny + nz
+    members = ns * ny + nz
     dma = pltpu.SemaphoreType.DMA
     vectors, hess = pl.pallas_call(
         functools.partial(kernel, grid, count),
@@ -541,14 +572,18 @@
             jax.ShapeDtypeStruct((STEPS, 40, CAP), F32),
             jax.ShapeDtypeStruct((STEPS, 23), F32),
         ),
-        in_specs=[anywhere] * 6,
+        in_specs=[anywhere] * 10,
         out_specs=(anywhere, pl.BlockSpec(memory_space=pltpu.VMEM)),
         scratch_shapes=[
             pltpu.VMEM((NVEC * 40, CAP), F32),
             pltpu.VMEM((5, 8, CAP), F32),
             pltpu.VMEM((8, CAP), F32),
             pltpu.VMEM((2, 5, 4, FACES), F32),
-            pltpu.VMEM((8, FACES), F32),
+            pltpu.VMEM((1, FACES), F32),
+            pltpu.VMEM((1, FACES), F32),
+            pltpu.VMEM((1, FACES), F32),
+            pltpu.VMEM((1, CELLS), F32),
+            pltpu.VMEM((2, FACES), jnp.int32),
             pltpu.VMEM((4, CAP), jnp.int32),
             pltpu.VMEM((STEPS, 40, CAP), F32),
             pltpu.VMEM((STEPS, 40, CAP), F32),
@@ -565,8 +600,8 @@
             pltpu.VMEM((2 * STEPS, 4, 40, CAP), F32),
             pltpu.VMEM((STEPS, 2, 40, CAP), F32),
             pltpu.VMEM((members, 8, CAP), F32),
-            pltpu.VMEM((STEPS + 1, members, 1, CAP), F32),
-            dma((6,)),
+            pltpu.VMEM((STEPS, members, 1, CAP), F32),
+            dma((10,)),
             dma((STEPS,)),
             dma((4,)),
             dma((4,)),
@@ -574,15 +609,26 @@
             dma((2 * STEPS, 4)),
             dma((STEPS, 2)),
             dma((STEPS, 2)),
-            dma((3,)),
-            dma((3,)),
-            dma((STEPS + 1, 3)),
-            dma((STEPS + 1, 3)),
+            dma((2,)),
+            dma((2,)),
+            dma((STEPS, 2)),
+            dma((STEPS, 2)),
         ],
         compiler_params=pltpu.CompilerParams(
-            collective_id=0, has_side_effects=True, vmem_limit_bytes=48 * 2**20
+            collective_id=0, has_side_effects=True, vmem_limit_bytes=60 * 2**20
         ),
-    )(halves(krylov).reshape(NVEC * 40, CAP), halves(limiter), halves(pseudo_diag), face_states, pack, send_list)
+    )(
+        halves(krylov).reshape(NVEC * 40, CAP),
+        halves(limiter),
+        halves(pseudo_diag),
+        face_states,
+        face_angle[None],
+        face_area[None],
+        slope_weight[None],
+        span_coupling[None],
+        face_cells,
+        send_list,
+    )
     vectors = jnp.swapaxes(vectors.reshape(STEPS, 5, 2, 4, CAP), 2, 3)
     return vectors.reshape(STEPS, 5, 4, CELLS), hess
 

time: 119 us -> 93.3 us (0.78)
  Pallas kernels: 112 us -> 90.5 us
  local copies, waits for them, and re-layouts: 5.15 us -> 2.04 us
    pallas_call x1, Pallas kernels: 112 us -> 90.5 us  [on_device(): pl.pallas_call(functools.partial(kernel, grid, count), out_shape=(jax.Sha...]
    unnamed x22 -> x4, local copies, waits for them, and re-layouts: 5.11 us -> 2.04 us
where the time goes in v1:
time: 93.3 us; the launch traced here: 93.1 us
  Pallas kernels  90.5 us (97%)
  local copies, waits for them, and re-layouts  2.04 us (2%)
    pallas_call x1, Pallas kernels, on_device(): pl.pallas_call(functools.partial(kernel, grid, count), out_shape=(jax.Sha...  90.5 us
    unnamed x4, local copies, waits for them, and re-layouts  2.04 us

profile of v1, /device:TPU:1, one launch (start us, length us, event | category | flops | bytes accessed | tf_op | source)
XLA Modules:
  0.0 93.1 jit_solution(11579473198420356377)
XLA Ops:
  0.6 90.5 %shard_map.113 = (f32[3,40,128]{2,1,0:T(8,128)}, f32[3,23]{1,0:T(4,128)}) custom-call(f32[800,128]{1,0:T(8,128)} %bitcast.24, f32[5,8,128]{2,1,0:T(8,128)} %bitcast.26, f32[8,128]{1,0:T(8,128)} %bitcast.27, f32[2,5,4,512]{3,2,1,0:T(4,128)} %fs_any.1, f32[1,512]{1,0:T(1,128)} %bitcast.28, f32[1,512]{1,0:T(1,128)} %bitcast.29, f32[1,512]{1,0:T(1,128)} %bitcast.30, ...), custom_call_target="tpu_custom_call" | custom-call | tf_op jit(solution)/shard_map/pallas_call | solution.py:569
  91.1 0.0 copy-start
  91.1 1.5 %copy.18 = f32[3,5,4,256]{3,2,1,0:T(4,128)} copy(f32[3,5,4,256]{3,2,1,0:T(4,128)} %bitcast.25) | data formatting | bytes 122880
  92.6 0.0 copy-done
  92.6 0.6 copy.19
Async XLA Ops:
  91.1 1.5 %copy-start = (f32[3,23]{1,0:T(4,128)S(1)}, f32[3,23]{1,0:T(4,128)}, u32[]{:S(2)}) copy-start(f32[3,23]{1,0:T(4,128)} %get-tuple-element.9) | copy-start | bytes 832

commit v2 on v1

--- a/solution.py
+++ b/solution.py
@@ -89,7 +89,7 @@
     coupling_any,
     cells_any,
     sl_any,
-    nv_any,
+    nv_ref,
     hess_ref,
     kv,
     limv,
@@ -101,7 +101,7 @@
     couplingv,
     cellsv,
     slv,
-    nvs,
+    m_slope,
     sv,
     rv,
     w_own,
@@ -118,7 +118,6 @@
     gbuf,
     abuf,
     load_sem,
-    out_sem,
     msg_send,
     msg_recv,
     nb_send,
@@ -333,8 +332,10 @@
         w_own[:, at + 512 : at + 512 + CAP] = (-hot).astype(BF16)
         w_sc[:, at + 1024 : at + 1024 + CAP] = hot.astype(BF16)
 
-    gram = sum_finish(gbuf, g_recv, 0)
-    sum_start(gbuf, g_send, g_recv, 1, gram)
+    def near(own):
+        return joined(dot_nn(operand(own), w_own[...]))
+
+    first_near = near([kv[40 * NVEC - 40 :, :]])
 
     for j in NEAR:
         when(exists[j], messages[j].wait_recv)
@@ -347,8 +348,7 @@
         w_nb[j, :, 0:CAP] = (-one_hot(CELLS, msg_in[j, 45:46, :].astype(jnp.int32))).astype(BF16)
         w_nb[j, :, CAP:] = one_hot(CELLS, msg_in[j, 44:45, :].astype(jnp.int32)).astype(BF16)
 
-    def jumps(own, number, copies):
-        near = joined(dot_nn(operand(own), w_own[...]))
+    def jumps(near, number, copies):
         ghost = [None] * 4
         foreign = [None] * 4
         for j in NEAR:
@@ -379,8 +379,8 @@
             e[4] * diag + cp4,
         ]
 
-    def state_part(own, number, copies):
-        e_int, e_gh, e_for = jumps(own, number, copies)
+    def state_part(near, number, copies):
+        e_int, e_gh, e_for = jumps(near, number, copies)
         jump_int, jump_gf = [], []
         for v in range(5):
             x = e_int[8 * v : 8 * v + 8]
@@ -399,12 +399,34 @@
         lhs = split2(jnp.concatenate(parts, axis=1)).astype(BF16)
         return packed_cells(joined(dot_nt(lhs, w_sc[...])))
 
-    def slope_part(own, number, copies):
-        d_int, d_gh, d_for = jumps(own, number, copies)
-        lhs = jnp.concatenate(
-            [d_int * pl_int[3:4, :], d_gh * pl_gf[0, 3:4, :], d_for * pl_gf[1, 3:4, :]], axis=1
-        )
-        return packed_cells(joined(dot_nt(split2(lhs).astype(BF16), w_own[...])))
+    def slope_matrices():
+        def store(index, faces, weights, cells):
+            hi = weights.astype(BF16)
+            lo = (weights - hi.astype(F32)).astype(BF16)
+            matrix = dot_nt(faces * hi, cells) + dot_nt(faces * lo, cells)
+            hi = matrix.astype(BF16)
+            m_slope[index, :, 0:CELLS] = hi
+            m_slope[index, :, CELLS:] = (matrix - hi.astype(F32)).astype(BF16)
+
+        for j in range(4):
+            g, f = (3 - j) * CAP, j * CAP
+            weights = jnp.concatenate([pl_gf[0, 3:4, g : g + CAP], pl_gf[1, 3:4, f : f + CAP]], axis=1)
+            cells = jnp.concatenate(
+                [w_own[:, 512 + g : 512 + g + CAP], w_own[:, 1024 + f : 1024 + f + CAP]], axis=1
+            )
+            store(j, w_nb[j], weights, cells)
+        weights = jnp.concatenate([pl_int[3:4, :], pl_gf[0, 3:4, :], pl_gf[1, 3:4, :]], axis=1)
+        store(4, w_own[...], weights, w_own[...])
+
+    def slope_near(own):
+        return dot_nn(operand(own), m_slope[4])
+
+    def slope_part(total, number, copies):
+        for j in NEAR:
+            when(exists[j], copies[3 - j].wait_recv)
+            total = total + dot_nn(operand([nbuf[number, j]]), m_slope[j])
+        total = joined(total)
+        return packed_cells(total[:, :CELLS] + total[:, CELLS:])
 
     row = iota((8, CAP), 0)
     layer = row & 3
@@ -442,13 +464,18 @@
     hess = []
     norms = []
     for m in range(STEPS):
-        state_terms = state_part(q, 2 * m, copies)
+        state_terms = state_part(near(q) if m else first_near, 2 * m, copies)
         if m == 0:
             loads[8].wait()
             loads[9].wait()
         slope_field = [limv[v] * state_terms[v] for v in range(5)]
         sv[m] = jnp.concatenate(slope_field, axis=0)
         slope_copies = send_field(sv.at[m], 2 * m + 1)
+        if m == 0:
+            slope_matrices()
+            gram = sum_finish(gbuf, g_recv, 0)
+            sum_start(gbuf, g_send, g_recv, 1, gram)
+        slope_own = slope_near(slope_field)
         for copy in span_copies:
             copy.wait_recv()
         local = []
@@ -458,6 +485,19 @@
             local.append(
                 pdv[...] * q[v] + coupling * (2.0 * q[v] - above - below) + state_terms[v]
             )
+        slope_terms = slope_part(slope_own, 2 * m + 1, slope_copies)
+        w = [local[v] - slope_terms[v] for v in range(5)]
+
+        terms = {i: product(basis(i), w) for i in range(NVEC)}
+        for i, vector in enumerate(done):
+            terms[NVEC + i] = product(vector, w)
+        if m:
+            terms[NVEC + m - 1] = product(q, w)
+            terms[22] = rr
+        if m == STEPS - 1:
+            terms[23] = product(w, w)
+        value = local_sums(terms)
+        sum_start(abuf.at[m], a_send.at[m], a_recv.at[m], 0, value)
         if m == 0:
             gram = sum_finish(gbuf, g_recv, 1) / count
             wide = jnp.concatenate(
@@ -474,21 +514,9 @@
                 scale = 1.0 / column[k : k + 1, :]
                 work = work - (column - jnp.where(row24[:, 0:1] == k, 1.0, 0.0)) * (pivot * scale)
             inverse = pltpu.roll(work, CAP - 32, 1)
-        slope_terms = slope_part(slope_field, 2 * m + 1, slope_copies)
-        w = [local[v] - slope_terms[v] for v in range(5)]
-
-        terms = {i: product(basis(i), w) for i in range(NVEC)}
-        for i, vector in enumerate(done):
-            terms[NVEC + i] = product(vector, w)
-        if m:
-            terms[NVEC + m - 1] = product(q, w)
-            terms[22] = rr
-        if m == STEPS - 1:
-            terms[23] = product(w, w)
-        value = local_sums(terms)
-        for stage in range(2):
-            sum_start(abuf.at[m], a_send.at[m], a_recv.at[m], stage, value)
-            value = sum_finish(abuf.at[m], a_recv.at[m], stage)
+        value = sum_finish(abuf.at[m], a_recv.at[m], 0)
+        sum_start(abuf.at[m], a_send.at[m], a_recv.at[m], 1, value)
+        value = sum_finish(abuf.at[m], a_recv.at[m], 1)
         value = value / count
         solved = jnp.sum(inverse * value, axis=1, keepdims=True)
         if m:
@@ -497,8 +525,7 @@
             beta = jnp.sqrt(norms[-1] + EPSILON)
             scale = 1.0 / beta
             last = [x * scale for x in q]
-            nvs[m - 1] = jnp.concatenate(last, axis=0)
-            pltpu.make_async_copy(nvs.at[m - 1], nv_any.at[m - 1], out_sem.at[m - 1]).start()
+            nv_ref[m - 1] = jnp.concatenate(last, axis=0)
             done.append(last)
             hess[-1] = jnp.where(iota((1, CAP), 1) == 22, beta, hess[-1])
             w = [x * scale for x in w]
@@ -537,8 +564,7 @@
     rr = ww * scale * scale + jnp.sum(inner, axis=0, keepdims=True)
     beta = jnp.sqrt(jnp.maximum(rr, 0.0) + EPSILON)
     scale = 1.0 / beta
-    nvs[STEPS - 1] = jnp.concatenate([x * scale for x in q], axis=0)
-    pltpu.make_async_copy(nvs.at[STEPS - 1], nv_any.at[STEPS - 1], out_sem.at[STEPS - 1]).start()
+    nv_ref[STEPS - 1] = jnp.concatenate([x * scale for x in q], axis=0)
     hess[-1] = jnp.where(iota((1, CAP), 1) == 22, beta, hess[-1])
     hess_ref[...] = jnp.concatenate(hess, axis=0)[:, 0:23]
 
@@ -549,8 +575,6 @@
         c.wait_send()
     for wait in unsent:
         wait()
-    for m in range(STEPS):
-        pltpu.make_async_copy(nvs.at[m], nv_any.at[m], out_sem.at[m]).wait()
 
 
 def on_device(grid, krylov, limiter, pseudo_diag, face_states, face_angle, face_area, slope_weight,
@@ -569,11 +593,11 @@
     vectors, hess = pl.pallas_call(
         functools.partial(kernel, grid, count),
         out_shape=(
-            jax.ShapeDtypeStruct((STEPS, 40, CAP), F32),
-            jax.ShapeDtypeStruct((STEPS, 23), F32),
+            pltpu.VMEM((STEPS, 40, CAP), F32),
+            pltpu.VMEM((STEPS, 23), F32),
         ),
         in_specs=[anywhere] * 10,
-        out_specs=(anywhere, pl.BlockSpec(memory_space=pltpu.VMEM)),
+        out_specs=(pl.BlockSpec(memory_space=pltpu.VMEM),) * 2,
         scratch_shapes=[
             pltpu.VMEM((NVEC * 40, CAP), F32),
             pltpu.VMEM((5, 8, CAP), F32),
@@ -585,7 +609,7 @@
             pltpu.VMEM((1, CELLS), F32),
             pltpu.VMEM((2, FACES), jnp.int32),
             pltpu.VMEM((4, CAP), jnp.int32),
-            pltpu.VMEM((STEPS, 40, CAP), F32),
+            pltpu.VMEM((5, CELLS, 2 * CELLS), BF16),
             pltpu.VMEM((STEPS, 40, CAP), F32),
             pltpu.VMEM((STEPS, 40, CAP), F32),
             pltpu.VMEM((CELLS, 1536), BF16),
@@ -602,7 +626,6 @@
             pltpu.VMEM((members, 8, CAP), F32),
             pltpu.VMEM((STEPS, members, 1, CAP), F32),
             dma((10,)),
-            dma((STEPS,)),
             dma((4,)),
             dma((4,)),
             dma((2 * STEPS, 4)),

time: 93.3 us -> 86.4 us (0.926)
  Pallas kernels: 90.5 us -> 84.4 us
    pallas_call x1, Pallas kernels: 90.5 us -> 84.4 us  [on_device(): pl.pallas_call(functools.partial(kernel, grid, count), out_shape=(pltpu.V...]
    unnamed x4 -> x2, local copies, waits for them, and re-layouts: 2.04 us -> 1.2 us
where the time goes in v2:
time: 86.4 us; the launch traced here: 86.2 us
  Pallas kernels  84.4 us (98%)
  local copies, waits for them, and re-layouts  1.2 us (1%)
    pallas_call x1, Pallas kernels, on_device(): pl.pallas_call(functools.partial(kernel, grid, count), out_shape=(pltpu.V...  84.4 us

profile of v2, /device:TPU:1, one launch (start us, length us, event | category | flops | bytes accessed | tf_op | source)
XLA Modules:
  0.0 86.2 jit_solution(6121736681159997075)
XLA Ops:
  0.6 84.4 %shard_map.113 = (f32[3,40,128]{2,1,0:T(8,128)S(1)}, f32[3,23]{1,0:T(4,128)S(1)}) custom-call(f32[800,128]{1,0:T(8,128)} %bitcast.25, f32[5,8,128]{2,1,0:T(8,128)} %bitcast.26, f32[8,128]{1,0:T(8,128)} %bitcast.27, f32[2,5,4,512]{3,2,1,0:T(4,128)} %fs_any.1, f32[1,512]{1,0:T(1,128)} %bitcast.28, f32[1,512]{1,0:T(1,128)} %bitcast.29, f32[1,512]{1,0:T(1,128)} %bitcast.30, ...), custom_call_target="tpu_custom_call" | custom-call | tf_op jit(solution)/shard_map/pallas_call | solution.py:593
  85.0 0.6 copy.18
  85.7 0.6 copy.19

commit v3 on v2

--- a/solution.py
+++ b/solution.py
@@ -128,6 +128,8 @@
     g_recv,
     a_send,
     a_recv,
+    meet_y,
+    meet_z,
 ):
     ns, ny, nz = grid
     nd = ny * nz
@@ -160,9 +162,16 @@
         ]
 
     barrier = pltpu.get_barrier_semaphore()
-    partners = [(s, dom_at(o)) for o in OFFSETS] + others(0) + others(1)
+    near_z = [(s, y * nz + lax.rem(z + k, nz)) for k in (nz - 2, nz - 1, 1, 2)]
+    near_y = [(s, lax.rem(y + k, ny) * nz + z) for k in range(1, ny)]
+    partners = [(s, dom_at(o)) for o in OFFSETS] + near_z + near_y
+    partners += [(lax.rem(s + k, ns), d) for k in range(1, ns)]
     for device in partners:
         pl.semaphore_signal(barrier, inc=1, device_id=device, device_id_type=MESH)
+
+    def greet(semaphore, devices):
+        for device in devices:
+            pl.semaphore_signal(semaphore, inc=1, device_id=device, device_id_type=MESH)
 
     pairs = (
         (fs_any, fsv),
@@ -196,7 +205,7 @@
 
     def send_field(src, number):
         copies = []
-        for j in NEAR:
+        for j in reversed(NEAR):
             copy = pltpu.make_async_remote_copy(
                 src_ref=src,
                 dst_ref=nbuf.at[number, 3 - j],
@@ -291,7 +300,7 @@
 
     first = send_field(k_any.at[pl.ds(40 * NVEC - 40, 40)], 0)
     messages = {}
-    for j in NEAR:
+    for j in reversed(NEAR):
         copy = pltpu.make_async_remote_copy(
             src_ref=msg_out.at[j],
             dst_ref=msg_in.at[j],
@@ -303,6 +312,8 @@
         when(exists[3 - j], copy.start)
         messages[j] = copy
     first_span = send_span(k_any.at[pl.ds(40 * NVEC - 40, 40)], 0)
+    circle = near_y + [near_z[0], near_z[3]]
+    greet(meet_y, circle)
 
     loads[6].wait()
     total = jnp.zeros((72, 72), F32)
@@ -317,7 +328,6 @@
     gram = rows[:, 0:24] + rows[:, 24:48] + rows[:, 48:72]
     gram = jnp.concatenate([gram, jnp.zeros((24, CAP - 24), F32)], axis=1)
     gram = gram[0:8] + pltpu.roll(gram[8:16], 32, 1) + pltpu.roll(gram[16:24], 64, 1)
-    sum_start(gbuf, g_send, g_recv, 0, gram)
 
     hot_a, hot_b = one_hot(CELLS, owner), one_hot(CELLS, other)
     w_own[:, 0:512] = (hot_a - hot_b).astype(BF16)
@@ -336,6 +346,11 @@
         return joined(dot_nn(operand(own), w_own[...]))
 
     first_near = near([kv[40 * NVEC - 40 :, :]])
+
+    pl.semaphore_wait(meet_y, len(circle))
+    far_z = [(s, y * nz + lax.rem(z + k, nz)) for k in (4, nz - 4)] if nz > 8 else []
+    greet(meet_z, far_z)
+    sum_start(gbuf, g_send, g_recv, 0, gram)
 
     for j in NEAR:
         when(exists[j], messages[j].wait_recv)
@@ -474,6 +489,8 @@
         if m == 0:
             slope_matrices()
             gram = sum_finish(gbuf, g_recv, 0)
+            if far_z:
+                pl.semaphore_wait(meet_z, len(far_z))
             sum_start(gbuf, g_send, g_recv, 1, gram)
         slope_own = slope_near(slope_field)
         for copy in span_copies:
@@ -498,6 +515,8 @@
             terms[23] = product(w, w)
         value = local_sums(terms)
         sum_start(abuf.at[m], a_send.at[m], a_recv.at[m], 0, value)
+        value = sum_finish(abuf.at[m], a_recv.at[m], 0)
+        sum_start(abuf.at[m], a_send.at[m], a_recv.at[m], 1, value)
         if m == 0:
             gram = sum_finish(gbuf, g_recv, 1) / count
             wide = jnp.concatenate(
@@ -514,8 +533,6 @@
                 scale = 1.0 / column[k : k + 1, :]
                 work = work - (column - jnp.where(row24[:, 0:1] == k, 1.0, 0.0)) * (pivot * scale)
             inverse = pltpu.roll(work, CAP - 32, 1)
-        value = sum_finish(abuf.at[m], a_recv.at[m], 0)
-        sum_start(abuf.at[m], a_send.at[m], a_recv.at[m], 1, value)
         value = sum_finish(abuf.at[m], a_recv.at[m], 1)
         value = value / count
         solved = jnp.sum(inverse * value, axis=1, keepdims=True)
@@ -636,6 +653,8 @@
             dma((2,)),
             dma((STEPS, 2)),
             dma((STEPS, 2)),
+            pltpu.SemaphoreType.REGULAR,
+            pltpu.SemaphoreType.REGULAR,
         ],
         compiler_params=pltpu.CompilerParams(
             collective_id=0, has_side_effects=True, vmem_limit_bytes=60 * 2**20

time: 86.4 us -> 83.3 us (0.964)
  Pallas kernels: 84.4 us -> 81.3 us
    pallas_call x1, Pallas kernels: 84.4 us -> 81.3 us  [on_device(): pl.pallas_call(functools.partial(kernel, grid, count), out_shape=(pltpu.V...]
where the time goes in v3:
time: 83.3 us; the launch traced here: 83.2 us
  Pallas kernels  81.3 us (98%)
  local copies, waits for them, and re-layouts  1.2 us (1%)
    pallas_call x1, Pallas kernels, on_device(): pl.pallas_call(functools.partial(kernel, grid, count), out_shape=(pltpu.V...  81.3 us

profile of v3, /device:TPU:1, one launch (start us, length us, event | category | flops | bytes accessed | tf_op | source)
XLA Modules:
  0.0 83.2 jit_solution(14414608167675656924)
XLA Ops:
  0.6 81.3 %shard_map.113 = (f32[3,40,128]{2,1,0:T(8,128)S(1)}, f32[3,23]{1,0:T(4,128)S(1)}) custom-call(f32[800,128]{1,0:T(8,128)} %bitcast.25, f32[5,8,128]{2,1,0:T(8,128)} %bitcast.26, f32[8,128]{1,0:T(8,128)} %bitcast.27, f32[2,5,4,512]{3,2,1,0:T(4,128)} %fs_any.1, f32[1,512]{1,0:T(1,128)} %bitcast.28, f32[1,512]{1,0:T(1,128)} %bitcast.29, f32[1,512]{1,0:T(1,128)} %bitcast.30, ...), custom_call_target="tpu_custom_call" | custom-call | tf_op jit(solution)/shard_map/pallas_call | solution.py:610
  82.0 0.6 copy.18
  82.6 0.6 copy.19

commit v4 on v3

--- a/solution.py
+++ b/solution.py
@@ -10,6 +10,7 @@
 MESH = pl.DeviceIdType.MESH
 OFFSETS = (-2, -1, 1, 2)
 NEAR = (1, 2, 0, 3)
+PACE = (0, 2, 5, 7, 10, 13, 16, 19, 20)
 EPSILON = 1e-06
 F32 = jnp.float32
 BF16 = jnp.bfloat16
@@ -130,6 +131,14 @@
     a_recv,
     meet_y,
     meet_z,
+    far_kv,
+    wv,
+    far_w,
+    far_r,
+    kv_send,
+    kv_recv,
+    w_send,
+    w_recv,
 ):
     ns, ny, nz = grid
     nd = ny * nz
@@ -197,6 +206,8 @@
             msg_in[j] = jnp.zeros((48, CAP), F32)
             for number in range(2 * STEPS):
                 nbuf[number, j] = jnp.zeros((40, CAP), F32)
+            far_kv[j] = jnp.zeros((NVEC * 40, CAP), F32)
+            far_w[j] = jnp.zeros((40, CAP), F32)
 
     def when(condition, action):
         @pl.when(condition)
@@ -234,6 +245,35 @@
         return copies
 
     unsent = []
+
+    def send_basis(part):
+        low, high = PACE[part], PACE[part + 1]
+        rows = pl.ds(40 * low, 40 * (high - low))
+        for j in reversed(NEAR):
+            copy = pltpu.make_async_remote_copy(
+                src_ref=kv.at[rows],
+                dst_ref=far_kv.at[3 - j, rows],
+                send_sem=kv_send.at[j],
+                recv_sem=kv_recv.at[3 - j],
+                device_id=(s, dom_at(OFFSETS[j])),
+                device_id_type=MESH,
+            )
+            when(exists[j], copy.start)
+
+    def send_product():
+        copies = {}
+        for j in reversed(NEAR):
+            copies[j] = pltpu.make_async_remote_copy(
+                src_ref=wv,
+                dst_ref=far_w.at[3 - j],
+                send_sem=w_send.at[j],
+                recv_sem=w_recv.at[3 - j],
+                device_id=(s, dom_at(OFFSETS[j])),
+                device_id_type=MESH,
+            )
+            when(exists[j], copies[j].start)
+        return copies
+
 
     def sum_start(buf, send, recv, stage, value):
         place = buf.at[starts[stage] + places[stage]]
@@ -316,6 +356,7 @@
     greet(meet_y, circle)
 
     loads[6].wait()
+    send_basis(0)
     total = jnp.zeros((72, 72), F32)
     for pair in range(20):
         rows = jnp.concatenate(
@@ -367,8 +408,12 @@
         ghost = [None] * 4
         foreign = [None] * 4
         for j in NEAR:
-            when(exists[j], copies[3 - j].wait_recv)
-            part = joined(dot_nn(operand([nbuf[number, j]]), w_nb[j]))
+            if copies is None:
+                block = far_r[j]
+            else:
+                when(exists[j], copies[3 - j].wait_recv)
+                block = nbuf[number, j]
+            part = joined(dot_nn(operand([block]), w_nb[j]))
             ghost[3 - j] = part[:, :CAP]
             foreign[j] = part[:, CAP:]
         return (
@@ -443,6 +488,19 @@
         total = joined(total)
         return packed_cells(total[:, :CELLS] + total[:, CELLS:])
 
+    def far_residual(j, copies, scale, wide):
+        when(exists[j], copies[3 - j].wait_recv)
+        arrived = pltpu.make_async_copy(far_kv.at[j], far_kv.at[j], kv_recv.at[j])
+        when(exists[j], arrived.wait)
+        out = []
+        for v in range(5):
+            rows = slice(8 * v, 8 * v + 8)
+            r = far_w[j, rows, :] * scale
+            for i in range(NVEC):
+                r = r - wide[i : i + 1, :] * far_kv[j, 40 * i + 8 * v : 40 * i + 8 * v + 8, :]
+            out.append(r - wide[NVEC : NVEC + 1, :] * (nbuf[2, j, rows, :] * scale))
+        return jnp.concatenate(out, axis=0)
+
     row = iota((8, CAP), 0)
     layer = row & 3
     loads[7].wait()
@@ -486,6 +544,8 @@
         slope_field = [limv[v] * state_terms[v] for v in range(5)]
         sv[m] = jnp.concatenate(slope_field, axis=0)
         slope_copies = send_field(sv.at[m], 2 * m + 1)
+        if m < 2:
+            send_basis(4 * m + 1)
         if m == 0:
             slope_matrices()
             gram = sum_finish(gbuf, g_recv, 0)
@@ -515,8 +575,16 @@
             terms[23] = product(w, w)
         value = local_sums(terms)
         sum_start(abuf.at[m], a_send.at[m], a_recv.at[m], 0, value)
+        if m == 1:
+            wv[...] = jnp.concatenate(w, axis=0)
+            product_copies = send_product()
+            unsent += [functools.partial(when, exists[j], c.wait_send) for j, c in product_copies.items()]
+        if m < 2:
+            send_basis(4 * m + 2)
         value = sum_finish(abuf.at[m], a_recv.at[m], 0)
         sum_start(abuf.at[m], a_send.at[m], a_recv.at[m], 1, value)
+        if m < 2:
+            send_basis(4 * m + 3)
         if m == 0:
             gram = sum_finish(gbuf, g_recv, 1) / count
             wide = jnp.concatenate(
@@ -560,9 +628,15 @@
         rv[m] = jnp.concatenate(r, axis=0)
         unsent += [functools.partial(when, exists[j], c.wait_send) for j, c in slope_copies.items()]
         if m + 1 < STEPS:
-            copies = send_field(rv.at[m], 2 * m + 2)
+            if m == 0:
+                copies = send_field(rv.at[m], 2 * m + 2)
+                unsent += [functools.partial(when, exists[j], c.wait_send) for j, c in copies.items()]
+                send_basis(4)
+            else:
+                copies = None
+                for j in NEAR:
+                    far_r[j] = far_residual(j, product_copies, scale, wide)
             span_copies = send_span(rv.at[m], m + 1)
-            unsent += [functools.partial(when, exists[j], c.wait_send) for j, c in copies.items()]
             unsent += [c.wait_send for c in span_copies]
             rr = product(r, r)
         q = r
@@ -588,6 +662,7 @@
     for j in range(4):
         when(exists[j], first[j].wait_send)
         when(exists[3 - j], messages[j].wait_send)
+        when(exists[j], pltpu.make_async_copy(kv, kv, kv_send.at[j]).wait)
     for c in first_span:
         c.wait_send()
     for wait in unsent:
@@ -655,6 +730,14 @@
             dma((STEPS, 2)),
             pltpu.SemaphoreType.REGULAR,
             pltpu.SemaphoreType.REGULAR,
+            pltpu.VMEM((4, NVEC * 40, CAP), F32),
+            pltpu.VMEM((40, CAP), F32),
+            pltpu.VMEM((4, 40, CAP), F32),
+            pltpu.VMEM((4, 40, CAP), F32),
+            dma((4,)),
+            dma((4,)),
+            dma((4,)),
+            dma((4,)),
         ],
         compiler_params=pltpu.CompilerParams(
             collective_id=0, has_side_effects=True, vmem_limit_bytes=60 * 2**20

time: 83.3 us -> 81.5 us (0.978)
  Pallas kernels: 81.3 us -> 79.5 us
    pallas_call x1, Pallas kernels: 81.3 us -> 79.5 us  [on_device(): pl.pallas_call(functools.partial(kernel, grid, count), out_shape=(pltpu.V...]
where the time goes in v4:
time: 81.5 us; the launch traced here: 81.4 us
  Pallas kernels  79.5 us (98%)
  local copies, waits for them, and re-layouts  1.2 us (1%)
    pallas_call x1, Pallas kernels, on_device(): pl.pallas_call(functools.partial(kernel, grid, count), out_shape=(pltpu.V...  79.5 us

profile of v4, /device:TPU:1, one launch (start us, length us, event | category | flops | bytes accessed | tf_op | source)
XLA Modules:
  0.0 81.4 jit_solution(17737998008048158690)
XLA Ops:
  0.6 79.5 %shard_map.113 = (f32[3,40,128]{2,1,0:T(8,128)S(1)}, f32[3,23]{1,0:T(4,128)S(1)}) custom-call(f32[800,128]{1,0:T(8,128)} %bitcast.25, f32[5,8,128]{2,1,0:T(8,128)} %bitcast.26, f32[8,128]{1,0:T(8,128)} %bitcast.27, f32[2,5,4,512]{3,2,1,0:T(4,128)} %fs_any.1, f32[1,512]{1,0:T(1,128)} %bitcast.28, f32[1,512]{1,0:T(1,128)} %bitcast.29, f32[1,512]{1,0:T(1,128)} %bitcast.30, ...), custom_call_target="tpu_custom_call" | custom-call | tf_op jit(solution)/shard_map/pallas_call | solution.py:685
  80.2 0.6 copy.18
  80.8 0.6 copy.19

commit v5 on v4

--- a/solution.py
+++ b/solution.py
@@ -10,7 +10,7 @@
 MESH = pl.DeviceIdType.MESH
 OFFSETS = (-2, -1, 1, 2)
 NEAR = (1, 2, 0, 3)
-PACE = (0, 2, 5, 7, 10, 13, 16, 19, 20)
+PACE = (0, 2, 5, 7, 10, 13, 16, 18, 19)
 EPSILON = 1e-06
 F32 = jnp.float32
 BF16 = jnp.bfloat16
@@ -206,7 +206,7 @@
             msg_in[j] = jnp.zeros((48, CAP), F32)
             for number in range(2 * STEPS):
                 nbuf[number, j] = jnp.zeros((40, CAP), F32)
-            far_kv[j] = jnp.zeros((NVEC * 40, CAP), F32)
+            far_kv[j] = jnp.zeros((NVEC * 40 - 40, CAP), F32)
             far_w[j] = jnp.zeros((40, CAP), F32)
 
     def when(condition, action):
@@ -496,8 +496,9 @@
         for v in range(5):
             rows = slice(8 * v, 8 * v + 8)
             r = far_w[j, rows, :] * scale
-            for i in range(NVEC):
+            for i in range(NVEC - 1):
                 r = r - wide[i : i + 1, :] * far_kv[j, 40 * i + 8 * v : 40 * i + 8 * v + 8, :]
+            r = r - wide[NVEC - 1 : NVEC, :] * nbuf[0, j, rows, :]
             out.append(r - wide[NVEC : NVEC + 1, :] * (nbuf[2, j, rows, :] * scale))
         return jnp.concatenate(out, axis=0)
 
@@ -662,7 +663,8 @@
     for j in range(4):
         when(exists[j], first[j].wait_send)
         when(exists[3 - j], messages[j].wait_send)
-        when(exists[j], pltpu.make_async_copy(kv, kv, kv_send.at[j]).wait)
+        sent = kv.at[pl.ds(0, NVEC * 40 - 40)]
+        when(exists[j], pltpu.make_async_copy(sent, sent, kv_send.at[j]).wait)
     for c in first_span:
         c.wait_send()
     for wait in unsent:
@@ -730,7 +732,7 @@
             dma((STEPS, 2)),
             pltpu.SemaphoreType.REGULAR,
             pltpu.SemaphoreType.REGULAR,
-            pltpu.VMEM((4, NVEC * 40, CAP), F32),
+            pltpu.VMEM((4, NVEC * 40 - 40, CAP), F32),
             pltpu.VMEM((40, CAP), F32),
             pltpu.VMEM((4, 40, CAP), F32),
             pltpu.VMEM((4, 40, CAP), F32),

time: 81.5 us -> 81.5 us (level)
  no operation moved by 1% of the time
where the time goes in v5:
time: 81.5 us; the launch traced here: 81.4 us
  Pallas kernels  79.5 us (98%)
  local copies, waits for them, and re-layouts  1.2 us (1%)
    pallas_call x1, Pallas kernels, on_device(): pl.pallas_call(functools.partial(kernel, grid, count), out_shape=(pltpu.V...  79.5 us

profile of v5, /device:TPU:1, one launch (start us, length us, event | category | flops | bytes accessed | tf_op | source)
XLA Modules:
  0.0 81.4 jit_solution(2613377941782449007)
XLA Ops:
  0.6 79.5 %shard_map.113 = (f32[3,40,128]{2,1,0:T(8,128)S(1)}, f32[3,23]{1,0:T(4,128)S(1)}) custom-call(f32[800,128]{1,0:T(8,128)} %bitcast.25, f32[5,8,128]{2,1,0:T(8,128)} %bitcast.26, f32[8,128]{1,0:T(8,128)} %bitcast.27, f32[2,5,4,512]{3,2,1,0:T(4,128)} %fs_any.1, f32[1,512]{1,0:T(1,128)} %bitcast.28, f32[1,512]{1,0:T(1,128)} %bitcast.29, f32[1,512]{1,0:T(1,128)} %bitcast.30, ...), custom_call_target="tpu_custom_call" | custom-call | tf_op jit(solution)/shard_map/pallas_call | solution.py:687
  80.2 0.6 copy.18
  80.8 0.6 copy.19
